TPU v7x, 32 devices: a whole 2x2x4 slice. The times are simulated.
32 devices in a mesh: dp: 16 (over z, y, x), tensor: 2 (over core).
Axes of the slice: x: 2, y: 2, z: 4, core: 2. Of those that a mesh axis runs over, the one named last changes fastest.
Arguments:
- tokens: bfloat16 [32768, 768], P('dp'), may hold values from -6 to 6
- lengths: int32 [64], P('dp'), may hold values from 64 to 512, as said below
- projections: bfloat16 [3, 768, 768], P(None, None, 'tensor'), may hold values from -0.21875 to 0.21875
- attention_bias: float32 [2, 768], P(None, 'tensor'), may hold values from -3 to 3
- output_weight: bfloat16 [768, 768], P('tensor'), may hold values from -1.75 to 1.75
- output_bias: float32 [768], replicated, may hold values from -3 to 3
- first_gain: float32 [768], replicated, may hold values from 0.4 to 1.6
- first_shift: float32 [768], replicated, may hold values from -3 to 3
- inner_weight: bfloat16 [768, 3072], P(None, 'tensor'), may hold values from -0.21875 to 0.21875
- inner_bias: float32 [3072], P('tensor'), may hold values from -3 to 3
- outer_weight: bfloat16 [3072, 768], P('tensor'), may hold values from -0.21875 to 0.21875
- outer_bias: float32 [768], replicated, may hold values from -3 to 3
- second_gain: float32 [768], replicated, may hold values from 0.4 to 1.6
- second_shift: float32 [768], replicated, may hold values from -3 to 3
- cotangent: bfloat16 [32768, 768], P('dp'), may hold values from -6 to 6
Outputs:
- layer_output: bfloat16 [32768, 768], P('dp')
- input_gradient: bfloat16 [32768, 768], P('dp')
- projections_gradient: float32 [3, 768, 768], P(None, None, 'tensor')
- attention_bias_gradient: float32 [2, 768], P(None, 'tensor')
- output_weight_gradient: float32 [768, 768], P('tensor')
- output_bias_gradient: float32 [768], replicated
- first_gain_gradient: float32 [768], replicated
- first_shift_gradient: float32 [768], replicated
- inner_weight_gradient: float32 [768, 3072], P(None, 'tensor')
- inner_bias_gradient: float32 [3072], P('tensor')
- outer_weight_gradient: float32 [3072, 768], P('tensor')
- outer_bias_gradient: float32 [768], replicated
- second_gain_gradient: float32 [768], replicated
- second_shift_gradient: float32 [768], replicated
Inputs may be any that keep to these rules, and one draw needn't show every extreme that they name: `lengths`: each sequence has 64 to 512 live tokens; one sequence has exactly 512.
All inputs are finite; a program needn't handle non-finite values.
Results may differ from a plain program's by a relative error of at most 0.023.
Values may be sent and summed in bfloat16 or wider, within the bound.
A program may use at most 192 MiB of HBM per device.

v0:
```python
import jax
import jax.numpy as jnp
from jax import lax
from jax.sharding import PartitionSpec as P

HEAD = 64


def layer_norm(values, gain_vector, shift_vector):
    centered = values - jnp.mean(values, axis=-1, keepdims=True)
    variance = jnp.mean(centered * centered, axis=-1, keepdims=True)
    inverse = lax.rsqrt(variance + 1e-06)
    normed = centered * inverse
    return (normed * gain_vector + shift_vector, normed, inverse)


def norm_backward(upstream, normed, inverse, gain_vector):
    scaled = upstream * gain_vector
    return inverse * (
        scaled
        - jnp.mean(scaled, axis=-1, keepdims=True)
        - normed * jnp.mean(scaled * normed, axis=-1, keepdims=True)
    )


def exact_gelu(values):
    return jax.nn.gelu(values, approximate=False)


def masked_scores(queries, keys_block, length_value):
    scores = jnp.einsum(
        "qhd,khd->hqk", queries, keys_block, preferred_element_type=jnp.float32
    ) * HEAD ** (-0.5)
    visible = jnp.arange(keys_block.shape[0], dtype=jnp.int32) < length_value
    return jnp.where(visible[None, None, :], scores, -1e30)


def attend(entry):
    queries, keys_block, values_block, length_value = entry
    scores = masked_scores(queries, keys_block, length_value)
    maximum = jnp.max(scores, axis=-1, keepdims=True)
    exponent = jnp.exp(scores - maximum)
    totals = jnp.sum(exponent, axis=-1, keepdims=True)
    weights_low = (exponent / totals).astype(jnp.bfloat16)
    mixed = jnp.einsum(
        "hqk,khd->qhd", weights_low, values_block, preferred_element_type=jnp.float32
    )
    return (mixed.astype(jnp.bfloat16), maximum + jnp.log(totals))


def attend_backward(entry):
    queries, keys_block, values_block, upstream, log_total, length_value = entry
    scores = masked_scores(queries, keys_block, length_value)
    weights_soft = jnp.exp(scores - log_total)
    grad_weights = jnp.einsum(
        "qhd,khd->hqk", upstream, values_block, preferred_element_type=jnp.float32
    )
    centre = jnp.sum(weights_soft * grad_weights, axis=-1, keepdims=True)
    grad_scores = (weights_soft * (grad_weights - centre)).astype(jnp.bfloat16)
    factor = HEAD ** (-0.5)
    grad_queries = (
        jnp.einsum("hqk,khd->qhd", grad_scores, keys_block, preferred_element_type=jnp.float32)
        * factor
    )
    grad_keys = (
        jnp.einsum("hqk,qhd->khd", grad_scores, queries, preferred_element_type=jnp.float32)
        * factor
    )
    grad_values = jnp.einsum(
        "hqk,qhd->khd",
        weights_soft.astype(jnp.bfloat16),
        upstream,
        preferred_element_type=jnp.float32,
    )
    return (grad_queries, grad_keys, grad_values)


def per_device(
    tokens,
    lengths,
    projections,
    attention_bias,
    output_weight,
    output_bias,
    first_gain,
    first_shift,
    inner_weight,
    inner_bias,
    outer_weight,
    outer_bias,
    second_gain,
    second_shift,
    cotangent,
):
    slot_count = lengths.shape[0]
    row_count = tokens.shape[0]
    slot_length = row_count // slot_count
    local_width = projections.shape[2]
    head_count = local_width // HEAD
    shaped = (slot_count, slot_length, head_count, HEAD)
    inputs = tokens.astype(jnp.float32)
    bias_rows = jnp.stack([attention_bias[0], jnp.zeros_like(attention_bias[0]), attention_bias[1]])
    projected = jnp.einsum("td,cde->cte", tokens, projections, preferred_element_type=jnp.float32)
    projected_low = (projected + bias_rows[:, None, :]).astype(jnp.bfloat16)
    queries = projected_low[0].reshape(shaped)
    keys_all = projected_low[1].reshape(shaped)
    values_all = projected_low[2].reshape(shaped)
    mixed, log_total = lax.map(attend, (queries, keys_all, values_all, lengths))
    mixed_low = mixed.reshape(row_count, local_width)
    attention = lax.psum(
        jnp.dot(mixed_low, output_weight, preferred_element_type=jnp.float32).astype(jnp.bfloat16),
        "tensor",
    ).astype(jnp.float32)
    first_out, first_normed, first_inverse = layer_norm(
        inputs + attention + output_bias, first_gain, first_shift
    )
    first_low = first_out.astype(jnp.bfloat16)
    before = jnp.dot(first_low, inner_weight, preferred_element_type=jnp.float32) + inner_bias
    after, gelu_pull = jax.vjp(exact_gelu, before)
    after_low = after.astype(jnp.bfloat16)
    feedforward = lax.psum(
        jnp.dot(after_low, outer_weight, preferred_element_type=jnp.float32).astype(jnp.bfloat16),
        "tensor",
    ).astype(jnp.float32)
    layer_output, second_normed, second_inverse = layer_norm(
        first_out + feedforward + outer_bias, second_gain, second_shift
    )
    upstream = cotangent.astype(jnp.float32)
    second_gain_gradient = jnp.sum(upstream * second_normed, axis=0)
    second_shift_gradient = jnp.sum(upstream, axis=0)
    grad_second = norm_backward(upstream, second_normed, second_inverse, second_gain)
    outer_bias_gradient = jnp.sum(grad_second, axis=0)
    grad_second_low = grad_second.astype(jnp.bfloat16)
    outer_weight_gradient = jnp.einsum(
        "tf,td->fd", after_low, grad_second_low, preferred_element_type=jnp.float32
    )
    grad_after = jnp.einsum(
        "td,fd->tf", grad_second_low, outer_weight, preferred_element_type=jnp.float32
    )
    (grad_before,) = gelu_pull(grad_after)
    grad_before_low = grad_before.astype(jnp.bfloat16)
    inner_bias_gradient = jnp.sum(grad_before_low.astype(jnp.float32), axis=0)
    inner_weight_gradient = jnp.einsum(
        "td,tf->df", first_low, grad_before_low, preferred_element_type=jnp.float32
    )
    back_first = lax.psum(
        jnp.einsum(
            "tf,df->td", grad_before_low, inner_weight, preferred_element_type=jnp.float32
        ).astype(jnp.bfloat16),
        "tensor",
    ).astype(jnp.float32)
    grad_first_out = grad_second + back_first
    first_gain_gradient = jnp.sum(grad_first_out * first_normed, axis=0)
    first_shift_gradient = jnp.sum(grad_first_out, axis=0)
    grad_first = norm_backward(grad_first_out, first_normed, first_inverse, first_gain)
    output_bias_gradient = jnp.sum(grad_first, axis=0)
    grad_first_low = grad_first.astype(jnp.bfloat16)
    output_weight_gradient = jnp.einsum(
        "tl,td->ld", mixed_low, grad_first_low, preferred_element_type=jnp.float32
    )
    grad_mixed = jnp.einsum(
        "td,ld->tl", grad_first_low, output_weight, preferred_element_type=jnp.float32
    ).astype(jnp.bfloat16)
    grad_queries, grad_keys, grad_values = lax.map(
        attend_backward,
        (queries, keys_all, values_all, grad_mixed.reshape(shaped), log_total, lengths),
    )
    grad_projected = jnp.stack([grad_queries, grad_keys, grad_values]).reshape(
        3, row_count, local_width
    )
    grad_projected_low = grad_projected.astype(jnp.bfloat16)
    grad_summed = jnp.sum(grad_projected_low.astype(jnp.float32), axis=1)
    attention_bias_gradient = jnp.stack([grad_summed[0], grad_summed[2]])
    projections_gradient = jnp.einsum(
        "td,cte->cde", tokens, grad_projected_low, preferred_element_type=jnp.float32
    )
    back_input = lax.psum(
        jnp.einsum(
            "cte,cde->td", grad_projected_low, projections, preferred_element_type=jnp.float32
        ).astype(jnp.bfloat16),
        "tensor",
    ).astype(jnp.float32)
    input_gradient = (grad_first + back_input).astype(jnp.bfloat16)
    (
        projections_gradient,
        attention_bias_gradient,
        output_weight_gradient,
        output_bias_gradient,
        first_gain_gradient,
        first_shift_gradient,
        inner_weight_gradient,
        inner_bias_gradient,
        outer_weight_gradient,
        outer_bias_gradient,
        second_gain_gradient,
        second_shift_gradient,
    ) = lax.psum(
        (
            projections_gradient,
            attention_bias_gradient,
            output_weight_gradient,
            output_bias_gradient,
            first_gain_gradient,
            first_shift_gradient,
            inner_weight_gradient,
            inner_bias_gradient,
            outer_weight_gradient,
            outer_bias_gradient,
            second_gain_gradient,
            second_shift_gradient,
        ),
        "dp",
    )
    return (
        layer_output.astype(jnp.bfloat16),
        input_gradient,
        projections_gradient,
        attention_bias_gradient,
        output_weight_gradient,
        output_bias_gradient,
        first_gain_gradient,
        first_shift_gradient,
        inner_weight_gradient,
        inner_bias_gradient,
        outer_weight_gradient,
        outer_bias_gradient,
        second_gain_gradient,
        second_shift_gradient,
    )


def solution(mesh):
    in_specs = (
        P("dp", None),
        P("dp"),
        P(None, None, "tensor"),
        P(None, "tensor"),
        P("tensor", None),
        P(),
        P(),
        P(),
        P(None, "tensor"),
        P("tensor"),
        P("tensor", None),
        P(),
        P(),
        P(),
        P("dp", None),
    )
    out_specs = (
        P("dp", None),
        P("dp", None),
        P(None, None, "tensor"),
        P(None, "tensor"),
        P("tensor", None),
        P(),
        P(),
        P(),
        P(None, "tensor"),
        P("tensor"),
        P("tensor", None),
        P(),
        P(),
        P(),
    )
    return jax.shard_map(
        per_device, mesh=mesh, in_specs=in_specs, out_specs=out_specs, check_vma=False
    )
```

profile of v0, /device:TPU:0, one launch (start us, length us, event | category | flops | bytes accessed | tf_op | source)
XLA Modules:
  0.0 840.6 jit_solution(17614791287883799962)
XLA Ops:
  8.3 6.7 fusion.69
  17.3 4.1 reshape_squeeze.9
  21.5 2.9 copy.51
  24.4 3.9 reshape_squeeze.10
  28.2 2.9 copy.52
  31.1 3.8 reshape_squeeze.11
  35.0 2.9 copy.53
  37.9 37.4 %while.26 = (s32[]{:T(128)}, bf16[4,512,6,64]{1,3,2,0:T(8,128)(2,1)}, f32[4,6,512,1]{2,1,3,0:T(8,128)}, bf16[4,512,6,64]{1,3,2,0:T(8,128)(2,1)}, s32[4]{0:T(128)...) while((s32[]{:T(128)}, bf16[4,512,6,64]{1,3,2,0:T(8,128)(2,1)}, ...), condition=%wide.region_3.4_spmd, body=%wide.region_0.3_spmd.sunk | while | flops 421721600 | bytes 20554340 | solution.py:108
  43.7 3.5 fusion.128
  53.1 3.5 fusion.128
  62.4 3.5 fusion.128
  71.8 3.5 fusion.128
  79.6 3.5 convolution_convert_fusion
  83.2 26.0 %all-reduce.8.cloned.1.call-done = bf16[2048,768]{1,0:T(8,128)(2,1)} async-done(((bf16[2048,768]{1,0:T(8,128)(2,1)}), bf16[2048,768]{1,0:T(8,128)(2,1)}) %all-reduce.8.cloned.1.call-update) | async-done | bytes 3145744 | tf_op jit(solution)/shard_map/psum | solution.py:110
  109.2 4.1 fusion.68
  116.2 34.4 %multiply_convert_fusion.1 = (bf16[2048,1536]{1,0:T(8,128)(2,1)S(1)}, f32[2048,1536]{1,0:T(8,128)}, f32[2048,1536]{1,0:T(8,128)}) fusion(f32[1536]{0:T(1024)S(1)} %copy-done.33, bf16[768,1536]{1,0:T(8,128)(2,1)S(1)} %copy-done, f32[768]{0:T(1024)S(1)} %copy-done.31, f32[768]{0:T(1024)S(1)} %copy-done.24, f32[2048]{0:T(1024)S(1)} %add_rsqrt_fusion.1, ...), kind=kOutput, calls=%fused_computation.65 | convolution fusion | flops 5053612032 | bytes 40139776 | tf_op jit(solution)/shard_map/dot_general | solution.py:118
  153.3 6.3 convolution_convert_fusion.2
  159.7 24.5 %all-reduce.10.cloned.1.call-done = bf16[2048,768]{1,0:T(8,128)(2,1)} async-done(((bf16[2048,768]{1,0:T(8,128)(2,1)}), bf16[2048,768]{1,0:T(8,128)(2,1)}) %all-reduce.10.cloned.1.call-update) | async-done | bytes 3145744 | tf_op jit(solution)/shard_map/psum | solution.py:121
  184.2 5.5 fusion.88
  191.6 3.6 fusion.66
  195.3 5.1 fusion.64
  200.3 20.5 %convert_reduce_fusion = (f32[1536]{0:T(1024)}, bf16[2048,1536]{1,0:T(8,128)(2,1)}) fusion(f32[2048,1536]{1,0:T(8,128)} %get-tuple-element.233, bf16[1536,768]{1,0:T(8,128)(2,1)} %param.29, f32[2048,768]{1,0:T(8,128)} %get-tuple-element.238, f32[2048,1536]{1,0:T(8,128)} %get-tuple-element.247, f32[1536]{0:T(1024)S(1)} %copy-done.33), kind=kOutput, calls=%fused_computation.63 | convolution fusion | flops 4886886912 | bytes 40120320 | tf_op jit(solution)/shard_map/td,fd->tf/dot_general | solution.py:137
  220.8 9.3 %convolution_convert_fusion.1 = bf16[2048,768]{1,0:T(8,128)(2,1)} fusion(bf16[2048,1536]{1,0:T(8,128)(2,1)} %get-tuple-element.249, bf16[768,1536]{1,0:T(8,128)(2,1)S(1)} %copy-done), kind=kOutput, calls=%fused_computation.111 | convolution fusion | flops 4833411072 | bytes 11796480 | tf_op jit(solution)/shard_map/tf,df->td/dot_general | solution.py:147
  230.2 24.5 %all-reduce.12.cloned.1.call-done = bf16[2048,768]{1,0:T(8,128)(2,1)} async-done(((bf16[2048,768]{1,0:T(8,128)(2,1)}), bf16[2048,768]{1,0:T(8,128)(2,1)}) %all-reduce.12.cloned.1.call-update) | async-done | bytes 3145744 | tf_op jit(solution)/shard_map/psum | solution.py:146
  254.6 9.9 %multiply_reduce_fusion.1 = (f32[768]{0:T(1024)S(1)}, f32[2048]{0:T(1024)S(1)}, f32[2048]{0:T(1024)S(1)}, f32[768]{0:T(1024)S(1)}, f32[768]{0:T(1024)S(1)}) fusion(f32[2048,768]{1,0:T(8,128)} %get-tuple-element.238, bf16[2048,768]{1,0:T(8,128)(2,1)} %all-reduce.12.cloned.1.call-done, f32[2048]{0:T(1024)S(1)} %add_rsqrt_fusion.1, ...), kind=kLoop, calls=%fused_computation.92 | loop fusion | flops 25159424 | bytes 15776768 | tf_op jit(solution)/shard_map/reduce_sum | solution.py:153
  264.6 5.5 fusion.87
  272.8 3.0 convolution_convert_fusion.3
  278.6 3.8 reshape.125
  282.4 2.9 copy.58
  285.3 64.3 %while.27 = (s32[]{:T(128)}, bf16[4,512,6,64]{1,3,2,0:T(8,128)(2,1)}, bf16[4,512,6,64]{1,3,2,0:T(8,128)(2,1)}, bf16[4,512,6,64]{1,3,2,0:T(8,128)(2,1)}, bf16[4,5...) while((s32[]{:T(128)}, ...), condition=%wide.region_17.18_spmd, body=%wide.region_15.17_spmd.sunk | while | flops 1030616576 | bytes 83856648 | solution.py:164
  289.4 3.2 multiply_reduce_fusion.7
  305.5 3.2 multiply_reduce_fusion.7
  321.6 3.2 multiply_reduce_fusion.7
  337.6 3.2 multiply_reduce_fusion.7
  356.4 3.8 copy.61
  360.2 3.8 stack.20
  366.6 3.8 copy.62
  370.4 3.8 stack.21
  376.9 8.4 %bitcast_convert_fusion = bf16[2048,768]{1,0:T(8,128)(2,1)} fusion(bf16[3,768,384]{2,1,0:T(8,128)(2,1)} %param.21, bf16[1,2048,384]{2,1,0:T(8,128)(2,1)} %copy.65, bf16[1,2048,384]{2,1,0:T(8,128)(2,1)} %copy.64, bf16[1,2048,384]{2,1,0:T(8,128)(2,1)S(1)} %copy.63), kind=kOutput, calls=%fused_computation.91 | convolution fusion | flops 3630170112 | bytes 9633792 | tf_op jit(solution)/shard_map/cte,cde->td/dot_general | solution.py:178
  385.5 12.5 %fusion.82 = f32[768,1536]{1,0:T(8,128)} fusion(bf16[2048,1536]{1,0:T(8,128)(2,1)} %get-tuple-element.249, f32[768]{0:T(1024)S(1)} %copy-done.31, f32[768]{0:T(1024)S(1)} %copy-done.24, bf16[2048,768]{1,0:T(8,128)(2,1)} %all-reduce.8.cloned.1.call-done, bf16[2048,768]{1,0:T(8,128)(2,1)} %param.19, f32[2048]{0:T(1024)S(1)} %add_rsqrt_fusion.1, ...), kind=kOutput, calls=%fused_computation.124 | convolution fusion | flops 4845993984 | bytes 17327104 | tf_op jit(solution)/shard_map/td,tf->df/dot_general | solution.py:143
  398.0 10.8 %fusion.79 = f32[1536,768]{1,0:T(8,128)} fusion(bf16[2048,1536]{1,0:T(8,128)(2,1)} %copy-done.36, f32[2048,768]{1,0:T(8,128)} %get-tuple-element.238), kind=kOutput, calls=%fused_computation.121 | convolution fusion | flops 4833411072 | bytes 17301504 | tf_op jit(solution)/shard_map/tf,td->fd/dot_general | solution.py:134
  408.8 5.3 fusion.76
  414.2 5.8 fusion.73
  422.2 81.5 %all-reduce = (f32[2,384]{1,0:T(2,128)}, f32[768]{0:T(1024)}, f32[768]{0:T(1024)}, f32[768]{0:T(1024)}, f32[1536]{0:T(1024)}, /*index=5*/f32[768]{0:T(1024)}, f32[768]{0:T(1024)}, f32[768]{0:T(1024)}) all-reduce(f32[2,384]{1,0:T(2,128)S(1)} %pad_maximum_fusion.2, ...), channel_id=1, replica_groups=mesh['dp'=16,'tensor'=2] {'dp'}, use_global_device_ids=true, to_apply=%region_21.22 | all-reduce | flops 6912 | bytes 55296 | tf_op jit(solution)/shard_map/psum | solution.py:197
  503.7 6.4 add_convert_fusion.2
  510.1 309.7 %all-reduce.16.cloned.1.call-done = (f32[3,768,384]{1,2,0:T(8,128)}, f32[384,768]{1,0:T(8,128)}, f32[768,1536]{1,0:T(8,128)}, f32[1536,768]{1,0:T(8,128)}) async-done(((f32[3,768,384]{1,2,0:T(8,128)}, f32[384,768]{1,0:T(8,128)}, f32[768,1536]{1,0:T(8,128)}, f32[1536,768]{1,0:T(8,128)}), (f32[3,768,384]{1,2,0:T(8,128)}, f32[384,768]{1,0:T(8,128)}, f32[768,1536]{1,0:T(8,128)}, ...) | async-done | bytes 14155792 | tf_op jit(solution)/shard_map/psum | solution.py:197
  819.9 5.2 copy.67
  826.1 5.5 copy.112
  (203 shorter events, 113.2 us)
Async XLA Ops:
  7.2 109.0 %copy-start = (bf16[768,1536]{1,0:T(8,128)(2,1)S(1)}, bf16[768,1536]{1,0:T(8,128)(2,1)}, u32[]{:S(2)}) copy-start(bf16[768,1536]{1,0:T(8,128)(2,1)} %param.27) | copy-start | bytes 7077892
  7.2 102.0 %all-reduce.8.cloned.1.call-start = ((), (), s32[]{:S(2)}) async-start(), calls=%async_computation | async-start | bytes 6291456 | tf_op jit(solution)/shard_map/psum | solution.py:110
  24.4 13.5 %copy-start.34 = (s32[4]{0:T(128)S(1)}, s32[4]{0:T(128)}, u32[]{:S(2)}) copy-start(s32[4]{0:T(128)} %param.20) | copy-start | bytes 52
  75.3 4.3 copy-start.21
  78.4 30.7 %copy-start.23 = (f32[768]{0:T(1024)S(1)}, f32[768]{0:T(1024)}, u32[]{:S(2)}) copy-start(f32[768]{0:T(1024)} %param.24) | copy-start | bytes 9220
  83.1 33.1 %copy-start.24 = (f32[768]{0:T(1024)S(1)}, f32[768]{0:T(1024)}, u32[]{:S(2)}) copy-start(f32[768]{0:T(1024)} %param.25) | copy-start | bytes 9220
  83.1 33.1 %copy-start.31 = (f32[768]{0:T(1024)S(1)}, f32[768]{0:T(1024)}, u32[]{:S(2)}) copy-start(f32[768]{0:T(1024)} %param.26) | copy-start | bytes 9220
  83.1 33.1 %copy-start.33 = (f32[1536]{0:T(1024)S(1)}, f32[1536]{0:T(1024)}, u32[]{:S(2)}) copy-start(f32[1536]{0:T(1024)} %param.28) | copy-start | bytes 18436
  83.1 101.1 %all-reduce.10.cloned.1.call-start = ((), (), s32[]{:S(2)}) async-start(), calls=%async_computation.1 | async-start | bytes 6291456 | tf_op jit(solution)/shard_map/psum | solution.py:121
  109.2 4.1 copy-start.3
  109.2 4.7 copy-start.6
  116.2 37.1 %copy-start.32 = (bf16[1536,768]{1,0:T(8,128)(2,1)S(1)}, bf16[1536,768]{1,0:T(8,128)(2,1)}, u32[]{:S(2)}) copy-start(bf16[1536,768]{1,0:T(8,128)(2,1)} %param.29) | copy-start | bytes 7077892
  150.6 2.7 copy-start.36
  153.3 30.9 %copy-start.29 = (f32[768]{0:T(1024)S(1)}, f32[768]{0:T(1024)}, u32[]{:S(2)}) copy-start(f32[768]{0:T(1024)} %param.30) | copy-start | bytes 9220
  159.7 95.0 %all-reduce.12.cloned.1.call-start = ((), (), s32[]{:S(2)}) async-start(), calls=%async_computation.2 | async-start | bytes 6291456 | tf_op jit(solution)/shard_map/psum | solution.py:146
  190.6 4.6 copy-start.30
  230.1 273.6 %all-reduce.14.cloned.1.call-start = ((), (), s32[]{:S(2)}) async-start(), calls=%async_computation.3 | async-start | bytes 6291456 | tf_op jit(solution)/shard_map/psum | solution.py:177
  254.6 9.9 %copy-start.4 = (bf16[2048,768]{1,0:T(8,128)(2,1)S(1)}, bf16[2048,768]{1,0:T(8,128)(2,1)}, u32[]{:S(2)}) copy-start(bf16[2048,768]{1,0:T(8,128)(2,1)} %param.19) | copy-start | bytes 9437188
  254.6 9.9 %copy-start.7 = (bf16[2048,768]{1,0:T(8,128)(2,1)S(1)}, bf16[2048,768]{1,0:T(8,128)(2,1)}, u32[]{:S(2)}) copy-start(bf16[2048,768]{1,0:T(8,128)(2,1)} %all-reduce.8.cloned.1.call-done) | copy-start | bytes 9437188
  254.6 10.0 %copy-start.10 = (bf16[2048,768]{1,0:T(8,128)(2,1)S(1)}, bf16[2048,768]{1,0:T(8,128)(2,1)}, u32[]{:S(2)}) copy-start(bf16[2048,768]{1,0:T(8,128)(2,1)} %all-reduce.12.cloned.1.call-done) | copy-start | bytes 9437188
  264.6 8.2 copy-start.22
  270.1 2.7 copy-start.2
  275.8 9.5 %copy-start.8 = (bf16[4,512,6,64]{1,3,2,0:T(8,128)(2,1)S(1)}, bf16[4,512,6,64]{1,3,2,0:T(8,128)(2,1)}, u32[]{:S(2)}) copy-start(bf16[4,512,6,64]{1,3,2,0:T(8,128)(2,1)} %get-tuple-element.448) | copy-start | bytes 4718596
  275.8 9.5 %copy-start.35 = (s32[4]{0:T(128)S(1)}, s32[4]{0:T(128)}, u32[]{:S(2)}) copy-start(s32[4]{0:T(128)} %param.20) | copy-start | bytes 52
  285.3 4.1 copy-start.11
  292.6 3.3 copy-start.16
  295.9 3.1 copy-start.19
  301.4 4.1 copy-start.11
  308.7 3.3 copy-start.16
  312.0 3.1 copy-start.19
  317.4 4.1 copy-start.11
  324.7 3.3 copy-start.16
  328.0 3.1 copy-start.19
  333.5 4.1 copy-start.11
  340.8 3.3 copy-start.16
  344.1 3.1 copy-start.19
  385.4 434.5 %all-reduce.16.cloned.1.call-start = ((), (), s32[]{:S(2)}) async-start(), calls=%async_computation.4 | async-start | bytes 28311552 | tf_op jit(solution)/shard_map/psum | solution.py:197
  398.0 10.8 %copy-start.15 = (bf16[48,8,4,512]{3,1,2,0:T(8,128)(2,1)S(1)}, bf16[48,8,4,512]{3,1,2,0:T(8,128)(2,1)}, u32[]{:S(2)}) copy-start(bf16[48,8,4,512]{3,1,2,0:T(8,128)(2,1)} %copy-done.14) | copy-start | bytes 4718596
  408.8 5.4 copy-start.5
  408.8 5.4 copy-start.12
  408.8 5.4 copy-start.13
  419.9 2.3 copy-start.26
  419.9 2.3 copy-start.27
  419.9 2.3 copy-start.28
  819.9 5.3 copy-start.20
  825.1 6.5 slice-start
  826.1 5.5 slice-start.1
  826.1 7.7 copy-start.1
  (11 other events, 18.4 us)
Sparse Core Ops, SparseCore 0:
  83.2 25.8 all-reduce.7
  159.8 24.3 all-reduce.9
  230.2 24.3 all-reduce.11
  385.5 24.3 all-reduce.13
  420.1 399.7 all-reduce.15
where the time goes:
time: 846 us; the launch traced here: 841 us
  waiting for transfers between devices  385 us (46%)
  matrix products  194 us (23%)
  local copies, waits for them, and re-layouts  98.2 us (12%)
  blocking collectives  81.5 us (10%)
  other arithmetic  67.5 us (8%)
  between operations  14.4 us (2%)
    psum x1, waiting for transfers between devices, per_device(): lax.psum((projections_gradient, attention_bias_gradient, output_weight_gr...  310 us
    psum x1, blocking collectives, per_device(): lax.psum((projections_gradient, attention_bias_gradient, output_weight_gr...  81.5 us
    dot_general x1, matrix products, per_device(): jnp.dot(first_low, inner_weight, preferred_element_type=jnp.float32)  34.4 us
    psum x1, waiting for transfers between devices, per_device(): lax.psum(jnp.dot(mixed_low, output_weight, preferred_element_type=jnp.flo...  26 us
    psum x1, waiting for transfers between devices, per_device(): lax.psum(jnp.dot(after_low, outer_weight, preferred_element_type=jnp.floa...  24.5 us
    psum x1, waiting for transfers between devices, per_device(): lax.psum(jnp.einsum('tf,df->td', grad_before_low, inner_weight, preferred...  24.5 us
    unnamed x73, local copies, waits for them, and re-layouts  22.6 us
    dot_general x1, matrix products, per_device(): jnp.einsum('td,fd->tf', grad_second_low, outer_weight, preferred_element_...  20.5 us
  transfers between devices with their start and end apart: 5, of which 4 were waited for; matrix products, arithmetic and copies ran while one was open for 5% of the time, Pallas kernels for 0%

commit v1 on v0

--- a/solution.py
+++ b/solution.py
@@ -118,9 +118,14 @@
     before = jnp.dot(first_low, inner_weight, preferred_element_type=jnp.float32) + inner_bias
     after, gelu_pull = jax.vjp(exact_gelu, before)
     after_low = after.astype(jnp.bfloat16)
-    feedforward = lax.psum(
-        jnp.dot(after_low, outer_weight, preferred_element_type=jnp.float32).astype(jnp.bfloat16),
-        "tensor",
+
+    def clear_the_column(field):
+        all_values = lax.all_gather(field, axis_name="tensor")
+        f_next = jnp.sum(all_values, 0)
+        return f_next
+
+    feedforward = clear_the_column(
+        jnp.dot(after_low, outer_weight, preferred_element_type=jnp.float32).astype(jnp.bfloat16)
     ).astype(jnp.float32)
     layer_output, second_normed, second_inverse = layer_norm(
         first_out + feedforward + outer_bias, second_gain, second_shift

time: 846 us -> 846 us (level)
    psum x1 -> x0, waiting for transfers between devices: 24.5 us -> none  [per_device(): lax.psum(jnp.dot(after_low, outer_weight, preferred_element_type=jnp.floa...]
    all_gather x0 -> x1, waiting for transfers between devices: none -> 18 us  [clear_the_column(): all_values = lax.all_gather(field, axis_name='tensor')]
where the time goes in v1:
time: 846 us; the launch traced here: 841 us
  waiting for transfers between devices  378 us (45%)
  matrix products  194 us (23%)
  local copies, waits for them, and re-layouts  98.2 us (12%)
  blocking collectives  81.6 us (10%)
  other arithmetic  73.9 us (9%)
  between operations  14.4 us (2%)
    psum x1, waiting for transfers between devices, per_device(): lax.psum((projections_gradient, attention_bias_gradient, output_weight_gr...  310 us
    psum x1, blocking collectives, per_device(): lax.psum((projections_gradient, attention_bias_gradient, output_weight_gr...  81.6 us
    dot_general x1, matrix products, per_device(): jnp.dot(first_low, inner_weight, preferred_element_type=jnp.float32)  34.4 us
    psum x1, waiting for transfers between devices, per_device(): lax.psum(jnp.dot(mixed_low, output_weight, preferred_element_type=jnp.flo...  26 us
    psum x1, waiting for transfers between devices, per_device(): lax.psum(jnp.einsum('tf,df->td', grad_before_low, inner_weight, preferred...  24.5 us
    unnamed x73, local copies, waits for them, and re-layouts  22.6 us
    dot_general x1, matrix products, per_device(): jnp.einsum('td,fd->tf', grad_second_low, outer_weight, preferred_element_...  20.5 us
    dot_general x8, matrix products, masked_scores(): jnp.einsum('qhd,khd->hqk', queries, keys_block, preferred_element_type=jn...  19 us
  transfers between devices with their start and end apart: 5, of which 4 were waited for; matrix products, arithmetic and copies ran while one was open for 5% of the time, Pallas kernels for 0%

profile of v1, /device:TPU:0, one launch (start us, length us, event | category | flops | bytes accessed | tf_op | source)
XLA Modules:
  0.0 840.5 jit_solution(1629226203529718726)
XLA Ops:
  8.3 6.7 fusion.69
  17.3 4.1 reshape_squeeze.9
  21.5 2.9 copy.51
  24.4 3.9 reshape_squeeze.10
  31.1 3.8 reshape_squeeze.11
  35.0 2.9 copy.53
  37.9 37.4 %while.26 = (s32[]{:T(128)}, bf16[4,512,6,64]{1,3,2,0:T(8,128)(2,1)}, f32[4,6,512,1]{2,1,3,0:T(8,128)}, bf16[4,512,6,64]{1,3,2,0:T(8,128)(2,1)}, s32[4]{0:T(128)...) while((s32[]{:T(128)}, bf16[4,512,6,64]{1,3,2,0:T(8,128)(2,1)}, ...), condition=%wide.region_3.4_spmd, body=%wide.region_0.3_spmd.sunk | while | flops 421721600 | bytes 20554340 | solution.py:108
  43.7 3.5 fusion.128
  53.1 3.5 fusion.128
  62.4 3.5 fusion.128
  71.8 3.5 fusion.128
  79.6 3.5 convolution_convert_fusion
  83.2 26.0 %all-reduce.7.cloned.1.call-done = bf16[2048,768]{1,0:T(8,128)(2,1)} async-done(((bf16[2048,768]{1,0:T(8,128)(2,1)}), bf16[2048,768]{1,0:T(8,128)(2,1)}) %all-reduce.7.cloned.1.call-update) | async-done | bytes 3145744 | tf_op jit(solution)/shard_map/psum | solution.py:110
  109.2 4.1 fusion.68
  116.2 34.4 %multiply_convert_fusion.1 = (bf16[2048,1536]{1,0:T(8,128)(2,1)S(1)}, f32[2048,1536]{1,0:T(8,128)}, f32[2048,1536]{1,0:T(8,128)}) fusion(f32[1536]{0:T(1024)S(1)} %copy-done.33, bf16[768,1536]{1,0:T(8,128)(2,1)S(1)} %copy-done, f32[768]{0:T(1024)S(1)} %copy-done.31, f32[768]{0:T(1024)S(1)} %copy-done.24, f32[2048]{0:T(1024)S(1)} %add_rsqrt_fusion.1, ...), kind=kOutput, calls=%fused_computation.65 | convolution fusion | flops 5053612032 | bytes 40139776 | tf_op jit(solution)/shard_map/dot_general | solution.py:118
  153.3 6.3 convolution_convert_fusion.2
  159.7 18.0 %all-gather.3.cloned.1.call-done = bf16[4096,768]{1,0:T(8,128)(2,1)} async-done(((bf16[2048,768]{1,0:T(8,128)(2,1)}), bf16[4096,768]{1,0:T(8,128)(2,1)}) %all-gather.3.cloned.1.call-update) | async-done | bytes 6291472 | tf_op jit(solution)/shard_map/all_gather | solution.py:123
  177.8 6.4 reduce_sum.176
  184.1 5.5 fusion.88
  191.6 3.6 fusion.66
  195.2 5.1 fusion.64
  200.2 20.5 %convert_reduce_fusion = (f32[1536]{0:T(1024)}, bf16[2048,1536]{1,0:T(8,128)(2,1)}) fusion(f32[2048,1536]{1,0:T(8,128)} %get-tuple-element.233, bf16[1536,768]{1,0:T(8,128)(2,1)} %param.29, f32[2048,768]{1,0:T(8,128)} %get-tuple-element.238, f32[2048,1536]{1,0:T(8,128)} %get-tuple-element.247, f32[1536]{0:T(1024)S(1)} %copy-done.33), kind=kOutput, calls=%fused_computation.63 | convolution fusion | flops 4886886912 | bytes 40120320 | tf_op jit(solution)/shard_map/td,fd->tf/dot_general | solution.py:142
  220.7 9.3 %convolution_convert_fusion.1 = bf16[2048,768]{1,0:T(8,128)(2,1)} fusion(bf16[2048,1536]{1,0:T(8,128)(2,1)} %get-tuple-element.249, bf16[768,1536]{1,0:T(8,128)(2,1)S(1)} %copy-done), kind=kOutput, calls=%fused_computation.111 | convolution fusion | flops 4833411072 | bytes 11796480 | tf_op jit(solution)/shard_map/tf,df->td/dot_general | solution.py:152
  230.1 24.5 %all-reduce.9.cloned.1.call-done = bf16[2048,768]{1,0:T(8,128)(2,1)} async-done(((bf16[2048,768]{1,0:T(8,128)(2,1)}), bf16[2048,768]{1,0:T(8,128)(2,1)}) %all-reduce.9.cloned.1.call-update) | async-done | bytes 3145744 | tf_op jit(solution)/shard_map/psum | solution.py:151
  254.5 9.9 %multiply_reduce_fusion.1 = (f32[768]{0:T(1024)S(1)}, f32[2048]{0:T(1024)S(1)}, f32[2048]{0:T(1024)S(1)}, f32[768]{0:T(1024)S(1)}, f32[768]{0:T(1024)S(1)}) fusion(f32[2048,768]{1,0:T(8,128)} %get-tuple-element.238, bf16[2048,768]{1,0:T(8,128)(2,1)} %all-reduce.9.cloned.1.call-done, f32[2048]{0:T(1024)S(1)} %add_rsqrt_fusion.1, ...), kind=kLoop, calls=%fused_computation.92 | loop fusion | flops 25159424 | bytes 15776768 | tf_op jit(solution)/shard_map/reduce_sum | solution.py:158
  264.5 5.5 fusion.87
  272.7 3.0 convolution_convert_fusion.3
  278.5 3.8 reshape.125
  282.3 2.9 copy.58
  285.2 64.3 %while.27 = (s32[]{:T(128)}, bf16[4,512,6,64]{1,3,2,0:T(8,128)(2,1)}, bf16[4,512,6,64]{1,3,2,0:T(8,128)(2,1)}, bf16[4,512,6,64]{1,3,2,0:T(8,128)(2,1)}, bf16[4,5...) while((s32[]{:T(128)}, ...), condition=%wide.region_17.18_spmd, body=%wide.region_15.17_spmd.sunk | while | flops 1030616576 | bytes 83856648 | solution.py:169
  289.4 3.2 multiply_reduce_fusion.7
  305.4 3.2 multiply_reduce_fusion.7
  321.5 3.2 multiply_reduce_fusion.7
  337.5 3.2 multiply_reduce_fusion.7
  356.4 3.8 copy.61
  360.1 3.8 stack.20
  366.5 3.8 copy.62
  370.3 3.8 stack.21
  376.9 8.4 %bitcast_convert_fusion = bf16[2048,768]{1,0:T(8,128)(2,1)} fusion(bf16[3,768,384]{2,1,0:T(8,128)(2,1)} %param.21, bf16[1,2048,384]{2,1,0:T(8,128)(2,1)} %copy.65, bf16[1,2048,384]{2,1,0:T(8,128)(2,1)} %copy.64, bf16[1,2048,384]{2,1,0:T(8,128)(2,1)S(1)} %copy.63), kind=kOutput, calls=%fused_computation.91 | convolution fusion | flops 3630170112 | bytes 9633792 | tf_op jit(solution)/shard_map/cte,cde->td/dot_general | solution.py:183
  385.4 12.5 %fusion.82 = f32[768,1536]{1,0:T(8,128)} fusion(bf16[2048,1536]{1,0:T(8,128)(2,1)} %get-tuple-element.249, f32[768]{0:T(1024)S(1)} %copy-done.31, f32[768]{0:T(1024)S(1)} %copy-done.24, bf16[2048,768]{1,0:T(8,128)(2,1)} %all-reduce.7.cloned.1.call-done, bf16[2048,768]{1,0:T(8,128)(2,1)} %param.19, f32[2048]{0:T(1024)S(1)} %add_rsqrt_fusion.1, ...), kind=kOutput, calls=%fused_computation.124 | convolution fusion | flops 4845993984 | bytes 17327104 | tf_op jit(solution)/shard_map/td,tf->df/dot_general | solution.py:148
  397.9 10.8 %fusion.79 = f32[1536,768]{1,0:T(8,128)} fusion(bf16[2048,1536]{1,0:T(8,128)(2,1)} %copy-done.36, f32[2048,768]{1,0:T(8,128)} %get-tuple-element.238), kind=kOutput, calls=%fused_computation.121 | convolution fusion | flops 4833411072 | bytes 17301504 | tf_op jit(solution)/shard_map/tf,td->fd/dot_general | solution.py:139
  408.7 5.3 fusion.76
  414.1 5.8 fusion.73
  422.1 81.6 %all-reduce = (f32[2,384]{1,0:T(2,128)}, f32[768]{0:T(1024)}, f32[768]{0:T(1024)}, f32[768]{0:T(1024)}, f32[1536]{0:T(1024)}, /*index=5*/f32[768]{0:T(1024)}, f32[768]{0:T(1024)}, f32[768]{0:T(1024)}) all-reduce(f32[2,384]{1,0:T(2,128)S(1)} %pad_maximum_fusion.2, ...), channel_id=1, replica_groups=mesh['dp'=16,'tensor'=2] {'dp'}, use_global_device_ids=true, to_apply=%region_21.22 | all-reduce | flops 6912 | bytes 55296 | tf_op jit(solution)/shard_map/psum | solution.py:202
  503.7 6.4 add_convert_fusion.2
  510.1 309.7 %all-reduce.13.cloned.1.call-done = (f32[3,768,384]{1,2,0:T(8,128)}, f32[384,768]{1,0:T(8,128)}, f32[768,1536]{1,0:T(8,128)}, f32[1536,768]{1,0:T(8,128)}) async-done(((f32[3,768,384]{1,2,0:T(8,128)}, f32[384,768]{1,0:T(8,128)}, f32[768,1536]{1,0:T(8,128)}, f32[1536,768]{1,0:T(8,128)}), (f32[3,768,384]{1,2,0:T(8,128)}, f32[384,768]{1,0:T(8,128)}, f32[768,1536]{1,0:T(8,128)}, ...) | async-done | bytes 14155792 | tf_op jit(solution)/shard_map/psum | solution.py:202
  819.8 5.2 copy.67
  826.1 5.5 copy.111
  (204 shorter events, 116.1 us)
Async XLA Ops:
  7.2 109.0 %copy-start = (bf16[768,1536]{1,0:T(8,128)(2,1)S(1)}, bf16[768,1536]{1,0:T(8,128)(2,1)}, u32[]{:S(2)}) copy-start(bf16[768,1536]{1,0:T(8,128)(2,1)} %param.27) | copy-start | bytes 7077892
  7.2 102.0 %all-reduce.7.cloned.1.call-start = ((), (), s32[]{:S(2)}) async-start(), calls=%async_computation | async-start | bytes 6291456 | tf_op jit(solution)/shard_map/psum | solution.py:110
  24.4 13.5 %copy-start.34 = (s32[4]{0:T(128)S(1)}, s32[4]{0:T(128)}, u32[]{:S(2)}) copy-start(s32[4]{0:T(128)} %param.20) | copy-start | bytes 52
  75.3 4.3 copy-start.21
  78.4 30.7 %copy-start.23 = (f32[768]{0:T(1024)S(1)}, f32[768]{0:T(1024)}, u32[]{:S(2)}) copy-start(f32[768]{0:T(1024)} %param.24) | copy-start | bytes 9220
  83.1 33.1 %copy-start.24 = (f32[768]{0:T(1024)S(1)}, f32[768]{0:T(1024)}, u32[]{:S(2)}) copy-start(f32[768]{0:T(1024)} %param.25) | copy-start | bytes 9220
  83.1 33.1 %copy-start.31 = (f32[768]{0:T(1024)S(1)}, f32[768]{0:T(1024)}, u32[]{:S(2)}) copy-start(f32[768]{0:T(1024)} %param.26) | copy-start | bytes 9220
  83.1 33.1 %copy-start.33 = (f32[1536]{0:T(1024)S(1)}, f32[1536]{0:T(1024)}, u32[]{:S(2)}) copy-start(f32[1536]{0:T(1024)} %param.28) | copy-start | bytes 18436
  83.1 94.6 %all-gather.3.cloned.1.call-start = ((), (), s32[]{:S(2)}) async-start(), calls=%async_computation.3 | async-start | bytes 9437184 | tf_op jit(solution)/shard_map/all_gather | solution.py:123
  109.2 4.1 copy-start.3
  109.2 4.7 copy-start.6
  116.2 37.1 %copy-start.32 = (bf16[1536,768]{1,0:T(8,128)(2,1)S(1)}, bf16[1536,768]{1,0:T(8,128)(2,1)}, u32[]{:S(2)}) copy-start(bf16[1536,768]{1,0:T(8,128)(2,1)} %param.29) | copy-start | bytes 7077892
  150.6 2.7 copy-start.36
  159.6 24.5 %copy-start.29 = (f32[768]{0:T(1024)S(1)}, f32[768]{0:T(1024)}, u32[]{:S(2)}) copy-start(f32[768]{0:T(1024)} %param.30) | copy-start | bytes 9220
  159.7 94.9 %all-reduce.9.cloned.1.call-start = ((), (), s32[]{:S(2)}) async-start(), calls=%async_computation.1 | async-start | bytes 6291456 | tf_op jit(solution)/shard_map/psum | solution.py:151
  190.6 4.6 copy-start.30
  230.0 273.7 %all-reduce.11.cloned.1.call-start = ((), (), s32[]{:S(2)}) async-start(), calls=%async_computation.2 | async-start | bytes 6291456 | tf_op jit(solution)/shard_map/psum | solution.py:182
  254.5 9.9 %copy-start.4 = (bf16[2048,768]{1,0:T(8,128)(2,1)S(1)}, bf16[2048,768]{1,0:T(8,128)(2,1)}, u32[]{:S(2)}) copy-start(bf16[2048,768]{1,0:T(8,128)(2,1)} %param.19) | copy-start | bytes 9437188
  254.5 9.9 %copy-start.7 = (bf16[2048,768]{1,0:T(8,128)(2,1)S(1)}, bf16[2048,768]{1,0:T(8,128)(2,1)}, u32[]{:S(2)}) copy-start(bf16[2048,768]{1,0:T(8,128)(2,1)} %all-reduce.7.cloned.1.call-done) | copy-start | bytes 9437188
  254.5 10.0 %copy-start.10 = (bf16[2048,768]{1,0:T(8,128)(2,1)S(1)}, bf16[2048,768]{1,0:T(8,128)(2,1)}, u32[]{:S(2)}) copy-start(bf16[2048,768]{1,0:T(8,128)(2,1)} %all-reduce.9.cloned.1.call-done) | copy-start | bytes 9437188
  264.5 8.2 copy-start.22
  270.0 2.7 copy-start.2
  275.7 9.5 %copy-start.8 = (bf16[4,512,6,64]{1,3,2,0:T(8,128)(2,1)S(1)}, bf16[4,512,6,64]{1,3,2,0:T(8,128)(2,1)}, u32[]{:S(2)}) copy-start(bf16[4,512,6,64]{1,3,2,0:T(8,128)(2,1)} %get-tuple-element.448) | copy-start | bytes 4718596
  275.7 9.5 %copy-start.35 = (s32[4]{0:T(128)S(1)}, s32[4]{0:T(128)}, u32[]{:S(2)}) copy-start(s32[4]{0:T(128)} %param.20) | copy-start | bytes 52
  285.2 4.1 copy-start.11
  292.5 3.3 copy-start.16
  295.8 3.1 copy-start.19
  301.3 4.1 copy-start.11
  308.6 3.3 copy-start.16
  311.9 3.1 copy-start.19
  317.4 4.1 copy-start.11
  324.6 3.3 copy-start.16
  327.9 3.1 copy-start.19
  333.4 4.1 copy-start.11
  340.7 3.3 copy-start.16
  344.0 3.1 copy-start.19
  385.3 434.5 %all-reduce.13.cloned.1.call-start = ((), (), s32[]{:S(2)}) async-start(), calls=%async_computation.4 | async-start | bytes 28311552 | tf_op jit(solution)/shard_map/psum | solution.py:202
  397.9 10.8 %copy-start.15 = (bf16[48,8,4,512]{3,1,2,0:T(8,128)(2,1)S(1)}, bf16[48,8,4,512]{3,1,2,0:T(8,128)(2,1)}, u32[]{:S(2)}) copy-start(bf16[48,8,4,512]{3,1,2,0:T(8,128)(2,1)} %copy-done.14) | copy-start | bytes 4718596
  408.7 5.4 copy-start.5
  408.7 5.4 copy-start.12
  408.7 5.4 copy-start.13
  419.8 2.3 copy-start.26
  419.8 2.3 copy-start.27
  419.8 2.3 copy-start.28
  819.8 5.3 copy-start.20
  825.1 6.5 slice-start
  826.1 5.5 slice-start.1
  826.1 7.7 copy-start.1
  (11 other events, 18.4 us)
Sparse Core Ops, SparseCore 0:
  83.2 25.8 all-reduce.6
  159.8 17.9 all-gather.2
  230.1 24.3 all-reduce.8
  385.4 24.3 all-reduce.10
  420.0 399.7 all-reduce.12
